TPU v7x, 512 devices: a whole 4x8x8 slice. The times are simulated.
512 devices in a mesh: pair: 64 (over z_lo, y, core), virt: 8 (over z_hi, x).
Axes of the slice: x: 4, y: 8, z: 8 (z_hi: 2, z_lo: 4; z = z_hi * 4 + z_lo), core: 2. Of those that a mesh axis runs over, the one named last changes fastest.
Arguments:
- amplitudes: bfloat16 [16384, 8192], P('pair', 'virt'), may hold values from -6 to 6
- amp_mask: int32 [16384, 64], P('pair', 'virt'), may hold values 0 or 1
- integrals: bfloat16 [64, 12, 128, 128], P('virt'), may hold values from -0.15625 to 0.15625
- int_rows: int32 [64, 12], P('virt'), may hold values from 0 to 63, all different within a row
- mirror_slot: int32 [4096, 4], P('pair'), may hold values from 0 to 3, each once within a row
Outputs:
- symmetric: bfloat16 [16384, 8192], P('pair', 'virt')
Inputs may be any that keep to these rules, and one draw needn't show every extreme that they name: `int_rows`: each row names 12 different input tiles, and every input tile is named by some row. `mirror_slot`: each row is a permutation of 0 to 3.
All inputs are finite; a program needn't handle non-finite values. No bound on the sum of `amp_mask` on one device may be relied on, other than what follows from the above.
Results may differ from a plain program's by a relative error of at most 0.0051.
Values may be sent and summed in bfloat16 or wider, within the bound.
A program may use at most 128 MiB of HBM per device.

v0:
```python
import jax
import jax.numpy as jnp
from jax import lax
from jax.sharding import PartitionSpec as P


def on_device(amplitudes, amp_mask, integrals, int_rows, mirror_slot):
    row_count, local_cols = amplitudes.shape
    tile_size = integrals.shape[2]
    q_local = local_cols // tile_size
    p_local, degree = int_rows.shape
    pair_count = lax.axis_size("pair")
    block_rows = row_count // pair_count
    out_cols = p_local * tile_size
    masked = (
        amplitudes.reshape(row_count, q_local, tile_size)
        * amp_mask[:, :, None].astype(jnp.bfloat16)
    ).reshape(row_count, local_cols)
    flat_slots = (
        jnp.arange(pair_count, dtype=jnp.int32)[:, None] * block_rows + mirror_slot
    ).reshape(row_count)
    piece = lax.all_gather(masked, "virt", axis=1, tiled=True)
    width = piece.shape[1]
    tile_count = width // tile_size
    wanted = jnp.arange(tile_count, dtype=jnp.int32)
    onehot = (int_rows[:, :, None] == wanted[None, None, :]).astype(jnp.bfloat16)
    weights = jnp.einsum("pkq,pkxy->qxpy", onehot, integrals, preferred_element_type=jnp.float32)
    weights = weights.astype(jnp.bfloat16).reshape(width, out_cols)
    ladder = jnp.dot(piece, weights, preferred_element_type=jnp.float32).astype(jnp.bfloat16)
    received = lax.all_to_all(
        ladder.reshape(pair_count, block_rows, out_cols),
        "pair",
        split_axis=0,
        concat_axis=0,
        tiled=True,
    )
    mirrored = jnp.take(received.reshape(row_count, out_cols), flat_slots, axis=0)
    flipped = mirrored.reshape(row_count, p_local, tile_size)[:, :, ::-1].reshape(
        row_count, out_cols
    )
    return (ladder.astype(jnp.float32) + flipped.astype(jnp.float32)).astype(jnp.bfloat16)


def solution(mesh):
    placed = (
        P("pair", "virt"),
        P("pair", "virt"),
        P("virt", None, None, None),
        P("virt", None),
        P("pair", None),
    )
    return jax.shard_map(
        on_device, mesh=mesh, in_specs=placed, out_specs=P("pair", "virt"), check_vma=False
    )
```

profile of v0, /device:TPU:1, one launch (start us, length us, event | category | flops | bytes accessed | tf_op | source)
XLA Modules:
  0.0 189.5 jit_solution(17280562966891013453)
XLA Ops:
  6.5 0.0 copy-start
  6.5 0.0 all-gather.2.cloned.1.call-start
  6.5 0.8 convert_element_type.26
  7.4 0.1 copy.8
  7.5 0.3 mul.22
  7.9 1.9 %bitcast_multiply_fusion = bf16[256,1024]{1,0:T(8,128)(2,1)} fusion(bf16[256,1024]{1,0:T(8,128)(2,1)} %param.5, bf16[32,8,8,128]{3,2,1,0:T(8,128)(2,1)S(1)} %bitcast.30), kind=kLoop, calls=%fused_computation.10 | loop fusion | flops 262144 | bytes 1572864 | tf_op jit(solution)/shard_map/mul | solution.py:16
  9.8 0.0 all-gather.2.cloned.1.call-update
  9.8 0.0 copy-done
  9.8 8.9 %convert_bitcast_fusion = bf16[64,128,8,128]{3,0,1,2:T(8,128)(2,1)} fusion(bf16[8,12,128,128]{3,2,1,0:T(8,128)(2,1)S(1)} %copy-done, s32[8,12]{1,0:T(8,128)} %param.8), kind=kOutput, calls=%fused_computation.4 | convolution fusion | flops 209721344 | bytes 19923328 | tf_op jit(solution)/shard_map/pkq,pkxy->qxpy/dot_general | solution.py:27
  18.7 18.6 %copy.10 = bf16[64,128,8,128]{3,2,1,0:T(8,128)(2,1)} copy(bf16[64,128,8,128]{3,0,1,2:T(8,128)(2,1)} %convert_bitcast_fusion) | data formatting | bytes 33554432 | tf_op jit(solution)/shard_map/convert_element_type | solution.py:28
  37.3 91.1 %all-gather.2.cloned.1.call-done = bf16[256,8192]{1,0:T(8,128)(2,1)} async-done(((bf16[256,1024]{1,0:T(8,128)(2,1)}), bf16[256,8192]{1,0:T(8,128)(2,1)}) %all-gather.2.cloned.1.call-update) | async-done | bytes 4194320 | tf_op jit(solution)/shard_map/all_gather | solution.py:22
  128.4 0.0 copy-start.1
  128.4 12.3 %fusion.4 = bf16[256,1024]{1,0:T(8,128)(2,1)} fusion(bf16[256,8192]{1,0:T(8,128)(2,1)} %all-gather.2.cloned.1.call-done, bf16[1024,8,8,128]{3,2,1,0:T(8,128)(2,1)} %bitcast.28), kind=kOutput, calls=%fused_computation.6 | convolution fusion | flops 4295229440 | bytes 21495808 | tf_op jit(solution)/shard_map/dot_general | solution.py:29
  140.7 2.0 %reshape.70 = bf16[64,4,1024]{2,1,0:T(4,128)(2,1)} reshape(bf16[256,1024]{1,0:T(8,128)(2,1)} %fusion.4) | data formatting | bytes 1048576 | tf_op jit(solution)/shard_map/reshape | solution.py:31
  142.7 9.5 %all-to-all-start = ((bf16[64,4,1024]{2,1,0:T(4,128)(2,1)}), bf16[64,4,1024]{2,1,0:T(4,128)(2,1)}, u32[]{:S(2)}, u32[]{:S(2)}) async-start(bf16[64,4,1024]{2,1,0:T(4,128)(2,1)} %reshape.70), calls=%async_computation | async-start | bytes 1048576 | tf_op jit(solution)/shard_map/all_to_all | solution.py:30
  152.2 0.0 copy-done.1
  152.3 0.1 copy.11
  152.4 0.1 reshape.72
  152.5 0.1 reshape.69
  152.6 17.1 %all-to-all-done = bf16[64,4,1024]{2,1,0:T(4,128)(2,1)} async-done(((bf16[64,4,1024]{2,1,0:T(4,128)(2,1)}), bf16[64,4,1024]{2,1,0:T(4,128)(2,1)}, u32[]{:S(2)}, u32[]{:S(2)}) %all-to-all-start) | async-done | bytes 524320 | tf_op jit(solution)/shard_map/all_to_all | solution.py:30
  169.8 2.0 %reshape.71 = bf16[256,1024]{1,0:T(8,128)(2,1)} reshape(bf16[64,4,1024]{2,1,0:T(4,128)(2,1)} %all-to-all-done) | data formatting | bytes 1048576 | tf_op jit(solution)/shard_map/reshape | solution.py:37
  171.7 3.5 %gather_fusion = bf16[256,1024]{1,0:T(8,128)(2,1)} fusion(bf16[256,1024]{1,0:T(8,128)(2,1)} %reshape.71, s32[1024]{0:T(1024)S(1)} %pad_clamp_fusion), kind=kCustom, calls=%fused_computation | custom fusion | bytes 1049600 | tf_op jit(solution)/shard_map/jit(_take)/gather | solution.py:37
  175.2 1.1 copy.16
  176.3 1.1 bitcast_select_fusion
  177.5 1.9 %rev.3 = bf16[256,8,128]{2,1,0:T(8,128)(2,1)} reverse(bf16[256,8,128]{2,1,0:T(8,128)(2,1)} %bitcast_select_fusion), dimensions={2} | reverse | bytes 1048576 | tf_op jit(solution)/shard_map/rev | solution.py:38
  179.4 1.1 convert.2
  180.6 2.1 %fusion.7 = bf16[256,1024]{1,0:T(8,128)(2,1)} fusion(f32[32,8,8,128]{3,2,1,0:T(8,128)S(1)} %convert.2, bf16[256,1024]{1,0:T(8,128)(2,1)} %fusion.4), kind=kLoop, calls=%fused_computation.8 | loop fusion | flops 786432 | bytes 2097152 | tf_op jit(solution)/shard_map/convert_element_type | solution.py:41
  (5 shorter events, 0.0 us)
Async XLA Ops:
  6.5 3.3 %copy-start = (bf16[8,12,128,128]{3,2,1,0:T(8,128)(2,1)S(1)}, bf16[8,12,128,128]{3,2,1,0:T(8,128)(2,1)}, u32[]{:S(2)}) copy-start(bf16[8,12,128,128]{3,2,1,0:T(8,128)(2,1)} %param.7) | copy-start | bytes 9437188
  6.5 121.8 %all-gather.2.cloned.1.call-start = ((), (), s32[]{:S(2)}) async-start(), calls=%async_computation.1 | async-start | bytes 4718592 | tf_op jit(solution)/shard_map/all_gather | solution.py:22
  128.4 23.9 %copy-start.1 = (s32[64,4]{0,1:T(4,128)S(1)}, s32[64,4]{0,1:T(4,128)}, u32[]{:S(2)}) copy-start(s32[64,4]{0,1:T(4,128)} %param.9) | copy-start | bytes 3076
  142.7 27.0 %all-to-all-start = ((bf16[64,4,1024]{2,1,0:T(4,128)(2,1)}), bf16[64,4,1024]{2,1,0:T(4,128)(2,1)}, u32[]{:S(2)}, u32[]{:S(2)}) async-start(bf16[64,4,1024]{2,1,0:T(4,128)(2,1)} %reshape.70), calls=%async_computation | async-start | bytes 1048576 | tf_op jit(solution)/shard_map/all_to_all | solution.py:30
Sparse Core Ops, SparseCore 0:
  10.6 117.7 all-gather.1
where the time goes:
time: 190 us
  waiting for transfers between devices  108 us (57%)
  local copies, waits for them, and re-layouts  29.9 us (16%)
  matrix products  21.2 us (11%)
  between operations  13.5 us (7%)
  starting transfers between devices  9.51 us (5%)
  other arithmetic  7.19 us (4%)
    all_gather x1, waiting for transfers between devices, on_device(): piece = lax.all_gather(masked, 'virt', axis=1, tiled=True)  91.1 us
    convert_element_type x1, local copies, waits for them, and re-layouts, on_device(): weights = weights.astype(jnp.bfloat16).reshape(width, out_cols)  18.6 us
    all_to_all x1, waiting for transfers between devices, on_device(): lax.all_to_all(ladder.reshape(pair_count, block_rows, out_cols), 'pair',...  17.1 us
    dot_general x1, matrix products, on_device(): jnp.dot(piece, weights, preferred_element_type=jnp.float32)  12.3 us
    all_to_all x1, starting transfers between devices, on_device(): lax.all_to_all(ladder.reshape(pair_count, block_rows, out_cols), 'pair',...  9.51 us
    dot_general x1, matrix products, on_device(): jnp.einsum('pkq,pkxy->qxpy', onehot, integrals, preferred_element_type=jn...  8.9 us
  transfers between devices with their start and end apart: 2, of which 2 were waited for; matrix products, arithmetic and copies ran while one was open for 15% of the time, Pallas kernels for 0%

commit v1 on v0

v1 whole, which is shorter than its diff:
```python
import jax
import jax.numpy as jnp
from jax import lax
from jax.experimental import pallas as pl
from jax.experimental.pallas import tpu as pltpu
from jax.sharding import PartitionSpec as P

MESH = pl.DeviceIdType.MESH
BF16, F32 = jnp.bfloat16, jnp.float32

TILE = 128
Q_LOCAL, P_LOCAL, DEG = 8, 8, 12
NX, NZH, NZL, NY, NC = 4, 2, 4, 8, 2
PEERS = NY * NC
BLK = 4
CHUNKS = NZL
ROWS = PEERS * BLK
HALF = 8
GROUP = HALF * BLK * P_LOCAL
PACK = P_LOCAL * BLK


def remote(src, dst, send, recv, to):
    return pltpu.make_async_remote_copy(
        src_ref=src, dst_ref=dst, send_sem=send, recv_sem=recv, device_id=to, device_id_type=MESH
    )


def kernel(
    amp_hbm, mask_hbm, int_hbm, rows_hbm, slot_hbm, out_hbm,
    x0, x1, x2, x3, lad, sent, got, amp, mask, weights, rows, slot, turn, swap, out,
    slot_wide, load_sem, store_sem, gs, gr, ms, mr, met,
):
    xs = (x0, x1, x2, x3)
    pair, virt = lax.axis_index("pair"), lax.axis_index("virt")
    zl, mine = pair // PEERS, lax.rem(pair, PEERS)
    y, core = mine // NC, lax.rem(mine, NC)
    zh, x = virt // NX, lax.rem(virt, NX)
    xr, xl, xo = lax.rem(x + 1, NX), lax.rem(x + 3, NX), lax.rem(x + 2, NX)
    zo = 1 - zh
    to_r, to_l, to_z = (pair, zh * NX + xr), (pair, zh * NX + xl), (pair, zo * NX + x)

    def flipped(k):
        return (zl, zl + 1 - 2 * lax.rem(zl, 2), lax.rem(zl + 2, 4), 3 - zl)[k]

    order = (3, 2, 1, 0)
    targets = [flipped(k) for k in order]

    barrier = pltpu.get_barrier_semaphore()
    y_peers = [(zl * PEERS + lax.rem(y + i, NY) * NC + core, virt) for i in range(1, NY)]
    z_peers = [
        (lax.rem(zl + i // NC, NZL) * PEERS + y * NC + lax.rem(core + i % NC, NC), virt)
        for i in range(1, NZL * NC)
    ]
    first = [to_r, to_l, to_z] + z_peers + y_peers
    for peer in first:
        pl.semaphore_signal(barrier, inc=1, device_id=peer, device_id_type=MESH)

    loads = [pltpu.make_async_copy(mask_hbm, mask, load_sem.at[0])]
    for n, target in enumerate(targets):
        part = pl.ds(pl.multiple_of(target * ROWS, ROWS), ROWS)
        loads.append(pltpu.make_async_copy(amp_hbm.at[part], amp.at[n], load_sem.at[1 + n]))
    loads.append(pltpu.make_async_copy(slot_hbm, slot, load_sem.at[5]))
    loads.append(pltpu.make_async_copy(rows_hbm, rows, load_sem.at[6]))
    loads.append(pltpu.make_async_copy(int_hbm, weights, load_sem.at[7]))
    for load in loads:
        load.start()

    pending = []

    def gather(n, i, first_tile, tiles):
        block = xs[n].at[pl.ds(first_tile, tiles)]
        return block, gs.at[n, i], gr.at[n, i]

    def send(n, i, first_tile, tiles, to):
        block, s, r = gather(n, i, first_tile, tiles)
        copy = remote(block, block, s, r, to)
        copy.start()
        pending.append(copy)

    def arrived(n, i, first_tile, tiles):
        block, s, r = gather(n, i, first_tile, tiles)
        remote(block, block, s, r, to_z).wait_recv()

    def tile(z_hi, at_x):
        return (z_hi * NX + at_x) * Q_LOCAL

    own, other = tile(zh, x), tile(zo, x)

    def masked(n):
        loads[1 + n].wait()
        part = pl.ds(pl.multiple_of(targets[n] * ROWS, ROWS), ROWS)
        keep = mask[part, :].astype(F32)
        for q in range(Q_LOCAL):
            a = amp[n, :, q * TILE : (q + 1) * TILE].astype(F32)
            xs[n][own + q] = (a * keep[:, q : q + 1]).astype(BF16)

    loads[0].wait()
    masked(0)
    pl.semaphore_wait(barrier, len(first))
    for n in range(CHUNKS):
        if n:
            masked(n)
        send(n, 2, own, Q_LOCAL, to_z)
        send(n, 0, own, Q_LOCAL, to_r)
        send(n, 1, own, Q_LOCAL, to_l)
    for peer in y_peers:
        pl.semaphore_signal(met, inc=1, device_id=peer, device_id_type=MESH)

    def grid(shape, axis):
        return lax.broadcasted_iota(jnp.int32, shape, axis)

    i, j = grid((GROUP, GROUP), 0), grid((GROUP, GROUP), 1)
    to_send = lax.rem(i // BLK, P_LOCAL) * (HALF * BLK) + (i // PACK) * BLK + lax.rem(i, BLK)
    turn[...] = jnp.where(j == to_send, 1.0, 0.0).astype(BF16)
    i, j = grid((TILE, TILE), 0), grid((TILE, TILE), 1)
    back = jnp.where(i + j == TILE - 1, 1.0, 0.0).astype(BF16)
    loads[5].wait()
    total = NZL * ROWS
    i, j = grid((total, NZL * PEERS), 0), grid((total, NZL * PEERS), 1)
    spread = jnp.where(i // BLK == j, 1.0, 0.0).astype(BF16)
    each = jnp.dot(spread, slot[...].astype(F32).astype(BF16), preferred_element_type=F32)
    i, j = grid((total, BLK), 0), grid((total, BLK), 1)
    column = jnp.sum(jnp.where(lax.rem(i, BLK) == j, each, 0.0), axis=1, keepdims=True)
    slot_wide[...] = jnp.broadcast_to(column, (total, TILE))
    for n in range(CHUNKS):
        for h in range(2):
            start = pl.multiple_of(targets[n] * ROWS + h * HALF * BLK, HALF * BLK)
            part = slot_wide[pl.ds(start, HALF * BLK), :]
            for half in range(2):
                i, j = grid((HALF * BLK, TILE), 0), grid((HALF * BLK, TILE), 1)
                offset = (j + half * TILE - (i // BLK) * PACK).astype(F32) - part
                for p in range(P_LOCAL):
                    swap[n, h, p * HALF * BLK : (p + 1) * HALF * BLK, half * TILE : (half + 1) * TILE] = (
                        jnp.where(offset == float(p * BLK), 1.0, 0.0).astype(BF16)
                    )
    loads[6].wait()
    loads[7].wait()

    def ladder(n):
        def one(p, carry):
            left = jnp.concatenate([xs[n][rows[p, k]] for k in range(DEG)], axis=1)
            acc = jnp.dot(left, weights[p], preferred_element_type=F32).astype(BF16)
            at = pl.ds(pl.multiple_of(p * HALF * BLK, HALF * BLK), HALF * BLK)
            lad[n, 0, at, :] = acc[: HALF * BLK]
            lad[n, 1, at, :] = acc[HALF * BLK :]
            return carry

        lax.fori_loop(0, P_LOCAL, one, 0)
        for h in range(2):
            packed = jnp.dot(turn[...], lad[n, h], preferred_element_type=F32).astype(BF16)
            sent[n, h * HALF : (h + 1) * HALF] = packed.reshape(HALF, PACK, TILE)

    def exchange(n):
        if order[n]:
            for i in range(PEERS):
                peer = (targets[n] * PEERS + i, virt)
                remote(sent.at[n, i], got.at[n, mine], ms.at[n], mr.at[n], peer).start()
        else:
            for i in range(1, PEERS):
                at = lax.rem(mine + i, PEERS)
                peer = (zl * PEERS + at, virt)
                remote(sent.at[n, at], got.at[n, mine], ms.at[n], mr.at[n], peer).start()
            got[n, mine] = sent[n, mine]

    def bytes_of(n):
        count = PEERS if order[n] else PEERS - 1
        part = pl.ds(0, count)
        return remote(sent.at[n, part], got.at[n, part], ms.at[n], mr.at[n], to_z)

    def combine(n):
        bytes_of(n).wait_recv()
        for h in range(2):
            block = got[n, h * HALF : (h + 1) * HALF].reshape(GROUP, TILE)
            mirrored = jnp.dot(swap[n, h], block, preferred_element_type=F32).astype(BF16)
            mirrored = jnp.dot(mirrored, back, preferred_element_type=F32)
            both = (lad[n, h].astype(F32) + mirrored).astype(BF16)
            for p in range(P_LOCAL):
                out[n, h * HALF * BLK : (h + 1) * HALF * BLK, p * TILE : (p + 1) * TILE] = (
                    both[p * HALF * BLK : (p + 1) * HALF * BLK]
                )
        part = pl.ds(pl.multiple_of(targets[n] * ROWS, ROWS), ROWS)
        pltpu.make_async_copy(out.at[n], out_hbm.at[part], store_sem.at[n]).start()

    for n in range(CHUNKS):
        arrived(n, 0, tile(zh, xl), 8)
        send(n, 3, tile(zh, xl), 4, to_r)
        arrived(n, 1, tile(zh, xr), 8)
        send(n, 4, tile(zh, xr) + 4, 4, to_l)
    for n in range(CHUNKS):
        arrived(n, 2, other, 8)
        send(n, 5, other, 8, to_r)
        send(n, 6, other, 8, to_l)
    pl.semaphore_wait(met, len(y_peers))

    def forward(n):
        arrived(n, 5, tile(zo, xl), 8)
        send(n, 7, tile(zo, xl), 4, to_r)
        arrived(n, 6, tile(zo, xr), 8)
        send(n, 8, tile(zo, xr) + 4, 4, to_l)

    def complete(n):
        arrived(n, 3, tile(zh, xo), 4)
        arrived(n, 4, tile(zh, xo) + 4, 4)
        arrived(n, 7, tile(zo, xo), 4)
        arrived(n, 8, tile(zo, xo) + 4, 4)

    forward(0)
    for n in range(CHUNKS):
        if n + 1 < CHUNKS:
            forward(n + 1)
        complete(n)
        ladder(n)
        exchange(n)
    for copy in pending:
        copy.wait_send()
    for n in range(CHUNKS):
        combine(n)
    for n in range(CHUNKS):
        bytes_of(n).wait_send()
        part = pl.ds(pl.multiple_of(targets[n] * ROWS, ROWS), ROWS)
        pltpu.make_async_copy(out.at[n], out_hbm.at[part], store_sem.at[n]).wait()


def on_device(amplitudes, amp_mask, integrals, int_rows, mirror_slot):
    hbm = pl.BlockSpec(memory_space=pl.ANY)
    total = CHUNKS * ROWS
    return pl.pallas_call(
        kernel,
        out_shape=jax.ShapeDtypeStruct((total, P_LOCAL * TILE), BF16),
        in_specs=[hbm] * 5,
        out_specs=hbm,
        scratch_shapes=[pltpu.VMEM((64, ROWS, TILE), BF16)] * CHUNKS
        + [
            pltpu.VMEM((CHUNKS, 2, GROUP, TILE), BF16),
            pltpu.VMEM((CHUNKS, PEERS, PACK, TILE), BF16),
            pltpu.VMEM((CHUNKS, PEERS, PACK, TILE), BF16),
            pltpu.VMEM((CHUNKS, ROWS, Q_LOCAL * TILE), BF16),
            pltpu.VMEM((total, Q_LOCAL), jnp.int32),
            pltpu.VMEM((P_LOCAL, DEG * TILE, TILE), BF16),
            pltpu.SMEM((P_LOCAL, DEG), jnp.int32),
            pltpu.VMEM((NZL * PEERS, BLK), jnp.int32),
            pltpu.VMEM((GROUP, GROUP), BF16),
            pltpu.VMEM((CHUNKS, 2, GROUP, GROUP), BF16),
            pltpu.VMEM((CHUNKS, ROWS, P_LOCAL * TILE), BF16),
            pltpu.VMEM((total, TILE), F32),
            pltpu.SemaphoreType.DMA((8,)),
            pltpu.SemaphoreType.DMA((CHUNKS,)),
            pltpu.SemaphoreType.DMA((CHUNKS, 9)),
            pltpu.SemaphoreType.DMA((CHUNKS, 9)),
            pltpu.SemaphoreType.DMA((CHUNKS,)),
            pltpu.SemaphoreType.DMA((CHUNKS,)),
            pltpu.SemaphoreType.REGULAR,
        ],
        compiler_params=pltpu.CompilerParams(
            collective_id=0, has_side_effects=True, vmem_limit_bytes=40 << 20
        ),
        name="ladder",
    )(amplitudes, amp_mask, integrals.reshape(P_LOCAL, DEG * TILE, TILE), int_rows, mirror_slot)


def solution(mesh):
    placed = (
        P("pair", "virt"),
        P("pair", "virt"),
        P("virt", None, None, None),
        P("virt", None),
        P("pair", None),
    )
    return jax.shard_map(
        on_device, mesh=mesh, in_specs=placed, out_specs=P("pair", "virt"), check_vma=False
    )
```

time: 190 us -> 71.2 us (0.37)
  waiting for transfers between devices: 108 us -> 0 us
  Pallas kernels: 0 us -> 64.9 us
  local copies, waits for them, and re-layouts: 29.9 us -> 6 us
  matrix products: 21.2 us -> 0 us
  between operations: 13.5 us -> 0.03 us
  starting transfers between devices: 9.51 us -> 0 us
  other arithmetic: 7.19 us -> 0 us
    all_gather x1 -> x0, waiting for transfers between devices: 91.1 us -> none  [on_device(): piece = lax.all_gather(masked, 'virt', axis=1, tiled=True)]
    pallas_call x0 -> x1, Pallas kernels: none -> 64.9 us  [on_device(): pl.pallas_call(kernel, out_shape=jax.ShapeDtypeStruct((total, P_LOCAL * T...]
    dot_general x2 -> x0, matrix products: 21.2 us -> none  [the longest x1 12.3 us: on_device(): jnp.dot(piece, weights, preferred_element_type=jnp.float32)]
    convert_element_type x2 -> x0, local copies, waits for them, and re-layouts: 18.7 us -> none  [the longest x1 18.6 us: on_device(): weights = weights.astype(jnp.bfloat16).reshape(width, out_cols)]
    all_to_all x1 -> x0, waiting for transfers between devices: 17.1 us -> none  [on_device(): lax.all_to_all(ladder.reshape(pair_count, block_rows, out_cols), 'pair',...]
    all_to_all x1 -> x0, starting transfers between devices: 9.51 us -> none  [on_device(): lax.all_to_all(ladder.reshape(pair_count, block_rows, out_cols), 'pair',...]
    unnamed x5 -> x9, local copies, waits for them, and re-layouts: 1.14 us -> 6 us
    reshape x4 -> x0, local copies, waits for them, and re-layouts: 4.2 us -> none  [the longest x1 2.03 us: on_device(): ladder.reshape(pair_count, block_rows, out_cols)]
  transfers between devices with their start and end apart: 2 -> 0, of which waited for: 2 -> 0; matrix products, arithmetic and copies ran while one was open for 15% -> 0% of each run, Pallas kernels for 0% -> 0%
where the time goes in v1:
time: 71.2 us; the launch traced here: 70.9 us
  Pallas kernels  64.9 us (91%)
  local copies, waits for them, and re-layouts  6 us (8%)
    pallas_call x1, Pallas kernels, on_device(): pl.pallas_call(kernel, out_shape=jax.ShapeDtypeStruct((total, P_LOCAL * T...  64.9 us
    unnamed x9, local copies, waits for them, and re-layouts  6 us

profile of v1, /device:TPU:1, one launch (start us, length us, event | category | flops | bytes accessed | tf_op | source)
XLA Modules:
  0.0 70.9 jit_solution(10112904894625122302)
XLA Ops:
  0.0 0.8 %copy.7.slot_hbm = s32[64,4]{1,0:T(8,128)S(1)} copy(s32[64,4]{0,1:T(4,128)} %param.9) | data formatting | bytes 2048 | tf_op args[4]
  0.8 0.8 %copy.6.mask_hbm = s32[256,8]{1,0:T(8,128)S(1)} copy(s32[256,8]{0,1:T(8,128)} %param.6) | data formatting | bytes 16384 | tf_op args[1]
  1.6 0.0 copy-start
  1.6 1.9 %copy-done = bf16[8,12,128,128]{3,2,1,0:T(8,128)(2,1)S(1)} copy-done((bf16[8,12,128,128]{3,2,1,0:T(8,128)(2,1)S(1)}, bf16[8,12,128,128]{3,2,1,0:T(8,128)(2,1)}, u32[]{:S(2)}) %copy-start) | copy-done | bytes 3145752
  3.5 0.0 copy-start.1
  3.5 1.0 %copy-done.1 = bf16[256,1024]{1,0:T(8,128)(2,1)S(1)} copy-done((bf16[256,1024]{1,0:T(8,128)(2,1)S(1)}, bf16[256,1024]{1,0:T(8,128)(2,1)}, u32[]{:S(2)}) %copy-start.1) | copy-done | bytes 524312
  4.5 0.0 copy-start.2
  4.5 0.7 copy-done.2
  5.2 64.9 %ladder.1 = bf16[256,1024]{1,0:T(8,128)(2,1)S(1)} custom-call(bf16[256,1024]{1,0:T(8,128)(2,1)S(1)} %copy-done.1, s32[256,8]{1,0:T(8,128)S(1)} %copy.6.mask_hbm, bf16[8,1536,128]{2,1,0:T(8,128)(2,1)S(1)} %bitcast.1, s32[8,12]{1,0:T(8,128)S(1)} %copy-done.2, s32[64,4]{1,0:T(8,128)S(1)} %copy.7.slot_hbm), custom_call_target="tpu_custom_call" | custom-call | tf_op jit(solution)/shard_map/ladder/pallas_call | solution.py:228
  70.1 0.8 %copy.9 = bf16[256,1024]{1,0:T(8,128)(2,1)} copy(bf16[256,1024]{1,0:T(8,128)(2,1)S(1)} %ladder.1) | data formatting | bytes 1048576
Async XLA Ops:
  1.6 1.9 %copy-start = (bf16[8,12,128,128]{3,2,1,0:T(8,128)(2,1)S(1)}, bf16[8,12,128,128]{3,2,1,0:T(8,128)(2,1)}, u32[]{:S(2)}) copy-start(bf16[8,12,128,128]{3,2,1,0:T(8,128)(2,1)} %param.7) | copy-start | bytes 9437188
  3.5 1.0 %copy-start.1 = (bf16[256,1024]{1,0:T(8,128)(2,1)S(1)}, bf16[256,1024]{1,0:T(8,128)(2,1)}, u32[]{:S(2)}) copy-start(bf16[256,1024]{1,0:T(8,128)(2,1)} %amp_hbm.1) | copy-start | bytes 1572868
  4.5 0.7 copy-start.2

commit v2 on v1

--- a/solution.py
+++ b/solution.py
@@ -27,9 +27,9 @@
 
 
 def kernel(
-    amp_hbm, mask_hbm, int_hbm, rows_hbm, slot_hbm, out_hbm,
-    x0, x1, x2, x3, lad, sent, got, amp, mask, weights, rows, slot, turn, swap, out,
-    slot_wide, load_sem, store_sem, gs, gr, ms, mr, met,
+    amp_hbm, mask_hbm, int_hbm, rows_hbm, slot_hbm, out,
+    x0, x1, x2, x3, lad, sent, got, amp, mask, weights, rows, slot, turn, swap,
+    slot_wide, keeps, load_sem, gs, gr, ms, mr, met,
 ):
     xs = (x0, x1, x2, x3)
     pair, virt = lax.axis_index("pair"), lax.axis_index("virt")
@@ -90,12 +90,13 @@
     def masked(n):
         loads[1 + n].wait()
         part = pl.ds(pl.multiple_of(targets[n] * ROWS, ROWS), ROWS)
-        keep = mask[part, :].astype(F32)
+        keep = keeps[part, :]
         for q in range(Q_LOCAL):
             a = amp[n, :, q * TILE : (q + 1) * TILE].astype(F32)
             xs[n][own + q] = (a * keep[:, q : q + 1]).astype(BF16)
 
     loads[0].wait()
+    keeps[...] = mask[...].astype(F32).T
     masked(0)
     pl.semaphore_wait(barrier, len(first))
     for n in range(CHUNKS):
@@ -119,7 +120,9 @@
     total = NZL * ROWS
     i, j = grid((total, NZL * PEERS), 0), grid((total, NZL * PEERS), 1)
     spread = jnp.where(i // BLK == j, 1.0, 0.0).astype(BF16)
-    each = jnp.dot(spread, slot[...].astype(F32).astype(BF16), preferred_element_type=F32)
+    each = lax.dot_general(
+        spread, slot[...].astype(F32).astype(BF16), (((1,), (1,)), ((), ())), preferred_element_type=F32
+    )
     i, j = grid((total, BLK), 0), grid((total, BLK), 1)
     column = jnp.sum(jnp.where(lax.rem(i, BLK) == j, each, 0.0), axis=1, keepdims=True)
     slot_wide[...] = jnp.broadcast_to(column, (total, TILE))
@@ -175,12 +178,11 @@
             mirrored = jnp.dot(swap[n, h], block, preferred_element_type=F32).astype(BF16)
             mirrored = jnp.dot(mirrored, back, preferred_element_type=F32)
             both = (lad[n, h].astype(F32) + mirrored).astype(BF16)
+            start = pl.multiple_of(targets[n] * ROWS + h * HALF * BLK, HALF * BLK)
             for p in range(P_LOCAL):
-                out[n, h * HALF * BLK : (h + 1) * HALF * BLK, p * TILE : (p + 1) * TILE] = (
-                    both[p * HALF * BLK : (p + 1) * HALF * BLK]
-                )
-        part = pl.ds(pl.multiple_of(targets[n] * ROWS, ROWS), ROWS)
-        pltpu.make_async_copy(out.at[n], out_hbm.at[part], store_sem.at[n]).start()
+                out[pl.ds(start, HALF * BLK), p * TILE : (p + 1) * TILE] = both[
+                    p * HALF * BLK : (p + 1) * HALF * BLK
+                ]
 
     for n in range(CHUNKS):
         arrived(n, 0, tile(zh, xl), 8)
@@ -218,8 +220,6 @@
         combine(n)
     for n in range(CHUNKS):
         bytes_of(n).wait_send()
-        part = pl.ds(pl.multiple_of(targets[n] * ROWS, ROWS), ROWS)
-        pltpu.make_async_copy(out.at[n], out_hbm.at[part], store_sem.at[n]).wait()
 
 
 def on_device(amplitudes, amp_mask, integrals, int_rows, mirror_slot):
@@ -227,25 +227,24 @@
     total = CHUNKS * ROWS
     return pl.pallas_call(
         kernel,
-        out_shape=jax.ShapeDtypeStruct((total, P_LOCAL * TILE), BF16),
+        out_shape=pltpu.VMEM((total, P_LOCAL * TILE), BF16),
         in_specs=[hbm] * 5,
-        out_specs=hbm,
+        out_specs=pl.BlockSpec(memory_space=pltpu.VMEM),
         scratch_shapes=[pltpu.VMEM((64, ROWS, TILE), BF16)] * CHUNKS
         + [
             pltpu.VMEM((CHUNKS, 2, GROUP, TILE), BF16),
             pltpu.VMEM((CHUNKS, PEERS, PACK, TILE), BF16),
             pltpu.VMEM((CHUNKS, PEERS, PACK, TILE), BF16),
             pltpu.VMEM((CHUNKS, ROWS, Q_LOCAL * TILE), BF16),
-            pltpu.VMEM((total, Q_LOCAL), jnp.int32),
+            pltpu.VMEM((Q_LOCAL, total), jnp.int32),
             pltpu.VMEM((P_LOCAL, DEG * TILE, TILE), BF16),
             pltpu.SMEM((P_LOCAL, DEG), jnp.int32),
-            pltpu.VMEM((NZL * PEERS, BLK), jnp.int32),
+            pltpu.VMEM((BLK, NZL * PEERS), jnp.int32),
             pltpu.VMEM((GROUP, GROUP), BF16),
             pltpu.VMEM((CHUNKS, 2, GROUP, GROUP), BF16),
-            pltpu.VMEM((CHUNKS, ROWS, P_LOCAL * TILE), BF16),
             pltpu.VMEM((total, TILE), F32),
+            pltpu.VMEM((total, Q_LOCAL), F32),
             pltpu.SemaphoreType.DMA((8,)),
-            pltpu.SemaphoreType.DMA((CHUNKS,)),
             pltpu.SemaphoreType.DMA((CHUNKS, 9)),
             pltpu.SemaphoreType.DMA((CHUNKS, 9)),
             pltpu.SemaphoreType.DMA((CHUNKS,)),
@@ -256,7 +255,18 @@
             collective_id=0, has_side_effects=True, vmem_limit_bytes=40 << 20
         ),
         name="ladder",
-    )(amplitudes, amp_mask, integrals.reshape(P_LOCAL, DEG * TILE, TILE), int_rows, mirror_slot)
+    )(
+        *(
+            pltpu.with_memory_space_constraint(a, pltpu.HBM)
+            for a in (
+                amplitudes,
+                amp_mask.T,
+                integrals.reshape(P_LOCAL, DEG * TILE, TILE),
+                int_rows,
+                mirror_slot.T,
+            )
+        )
+    )
 
 
 def solution(mesh):

time: 71.2 us -> 65.4 us (0.919)
  local copies, waits for them, and re-layouts: 6 us -> 0.8 us
    unnamed x9 -> x1, local copies, waits for them, and re-layouts: 6 us -> 0.8 us
where the time goes in v2:
time: 65.4 us; the launch traced here: 65.2 us
  Pallas kernels  64.4 us (98%)
  local copies, waits for them, and re-layouts  0.8 us (1%)
    pallas_call x1, Pallas kernels, on_device(): pl.pallas_call(kernel, out_shape=pltpu.VMEM((total, P_LOCAL * TILE), BF16...  64.4 us

profile of v2, /device:TPU:1, one launch (start us, length us, event | category | flops | bytes accessed | tf_op | source)
XLA Modules:
  0.0 65.2 jit_solution(9693940468132098778)
XLA Ops:
  0.0 64.4 %ladder.1 = bf16[256,1024]{1,0:T(8,128)(2,1)S(1)} custom-call(bf16[256,1024]{1,0:T(8,128)(2,1)} %amp_hbm.1, s32[8,256]{1,0:T(8,128)} %bitcast.4, bf16[8,1536,128]{2,1,0:T(8,128)(2,1)} %bitcast.3, s32[8,12]{1,0:T(8,128)} %rows_hbm.1, s32[4,64]{1,0:T(4,128)} %bitcast.5), custom_call_target="tpu_custom_call" | custom-call | tf_op jit(solution)/shard_map/ladder/pallas_call | solution.py:228
  64.4 0.8 %copy.7 = bf16[256,1024]{1,0:T(8,128)(2,1)} copy(bf16[256,1024]{1,0:T(8,128)(2,1)S(1)} %ladder.1) | data formatting | bytes 1048576

commit v3 on v2

v3 whole, which is shorter than its diff:
```python
import jax
import jax.numpy as jnp
from jax import lax
from jax.experimental import pallas as pl
from jax.experimental.pallas import tpu as pltpu
from jax.sharding import PartitionSpec as P

MESH = pl.DeviceIdType.MESH
BF16, F32 = jnp.bfloat16, jnp.float32

TILE = 128
Q_LOCAL, P_LOCAL, DEG = 8, 8, 12
NX, NZH, NZL, NY, NC = 4, 2, 4, 8, 2
PEERS = NY * NC
BLK = 4
HALF = 8
RUN = HALF * BLK
GROUP = RUN * P_LOCAL
PACK = P_LOCAL * BLK
GROUPS = NZL * PEERS // HALF
PLAN = ((3, (0, 1)), (2, (0, 1)), (1, (0, 1)), (0, (1,)), (0, (0,)))
CHUNKS = len(PLAN)
FIRST = [sum(len(c[1]) for c in PLAN[:n]) for n in range(CHUNKS)]


def remote(src, dst, send, recv, to):
    return pltpu.make_async_remote_copy(
        src_ref=src, dst_ref=dst, send_sem=send, recv_sem=recv, device_id=to, device_id_type=MESH
    )


def kernel(
    amp_hbm, mask_hbm, int_hbm, rows_hbm, slot_hbm, out, *scratch
):
    xs, amps, scratch = scratch[:CHUNKS], scratch[CHUNKS : 2 * CHUNKS], scratch[2 * CHUNKS :]
    lad, sent, got, mask, weights, rows, slot, turn, swap = scratch[:9]
    slot_wide, keeps, load_sem, gs, gr, ms, mr, met = scratch[9:]
    pair, virt = lax.axis_index("pair"), lax.axis_index("virt")
    zl, mine = pair // PEERS, lax.rem(pair, PEERS)
    y, core = mine // NC, lax.rem(mine, NC)
    zh, x = virt // NX, lax.rem(virt, NX)
    xr, xl, xo = lax.rem(x + 1, NX), lax.rem(x + 3, NX), lax.rem(x + 2, NX)
    zo = 1 - zh
    to_r, to_l, to_z = (pair, zh * NX + xr), (pair, zh * NX + xl), (pair, zo * NX + x)

    def flipped(k):
        return (zl, zl + 1 - 2 * lax.rem(zl, 2), lax.rem(zl + 2, 4), 3 - zl)[k]

    near = y // (NY // 2)

    def group_of(n, g):
        k, halves = PLAN[n]
        return flipped(k) * 2 + (near if halves[g] == 0 else 1 - near)

    def first_group(n):
        return group_of(n, 0) if len(PLAN[n][1]) == 1 else flipped(PLAN[n][0]) * 2

    def groups(n):
        return [first_group(n) + g for g in range(len(PLAN[n][1]))]

    def rows_of(n):
        size = RUN * len(PLAN[n][1])
        return pl.ds(pl.multiple_of(first_group(n) * RUN, RUN), size)

    barrier = pltpu.get_barrier_semaphore()
    y_peers = [(zl * PEERS + lax.rem(y + i, NY) * NC + core, virt) for i in range(1, NY)]
    z_peers = [
        (lax.rem(zl + i // NC, NZL) * PEERS + y * NC + lax.rem(core + i % NC, NC), virt)
        for i in range(1, NZL * NC)
    ]
    first = [to_r, to_l, to_z] + z_peers + y_peers
    for peer in first:
        pl.semaphore_signal(barrier, inc=1, device_id=peer, device_id_type=MESH)

    loads = [pltpu.make_async_copy(mask_hbm, mask, load_sem.at[0])]
    for n in range(CHUNKS):
        loads.append(pltpu.make_async_copy(amp_hbm.at[rows_of(n)], amps[n], load_sem.at[1 + n]))
    loads.append(pltpu.make_async_copy(slot_hbm, slot, load_sem.at[CHUNKS + 1]))
    loads.append(pltpu.make_async_copy(rows_hbm, rows, load_sem.at[CHUNKS + 2]))
    loads.append(pltpu.make_async_copy(int_hbm, weights, load_sem.at[CHUNKS + 3]))
    for load in loads:
        load.start()

    pending = []

    def gather(n, i, first_tile, tiles):
        block = xs[n].at[pl.ds(first_tile, tiles)]
        return block, gs.at[n, i], gr.at[n, i]

    def send(n, i, first_tile, tiles, to):
        block, s, r = gather(n, i, first_tile, tiles)
        copy = remote(block, block, s, r, to)
        copy.start()
        pending.append(copy)

    def arrived(n, i, first_tile, tiles):
        block, s, r = gather(n, i, first_tile, tiles)
        remote(block, block, s, r, to_z).wait_recv()

    def tile(z_hi, at_x):
        return (z_hi * NX + at_x) * Q_LOCAL

    own, other = tile(zh, x), tile(zo, x)

    def masked(n):
        loads[1 + n].wait()
        keep = keeps[rows_of(n), :]
        for q in range(Q_LOCAL):
            a = amps[n][:, q * TILE : (q + 1) * TILE].astype(F32)
            xs[n][own + q] = (a * keep[:, q : q + 1]).astype(BF16)

    loads[0].wait()
    keeps[...] = mask[...].astype(F32).T
    masked(0)
    pl.semaphore_wait(barrier, len(first))

    def own_x(n):
        send(n, 0, own, Q_LOCAL, to_r)
        send(n, 1, own, Q_LOCAL, to_l)

    def own_z(n):
        send(n, 2, own, Q_LOCAL, to_z)

    def pass_own(n):
        arrived(n, 0, tile(zh, xl), 8)
        send(n, 3, tile(zh, xl), 4, to_r)
        arrived(n, 1, tile(zh, xr), 8)
        send(n, 4, tile(zh, xr) + 4, 4, to_l)

    def cross(n):
        arrived(n, 2, other, 8)
        send(n, 5, other, 8, to_r)
        send(n, 6, other, 8, to_l)

    def forward(n):
        arrived(n, 5, tile(zo, xl), 8)
        send(n, 7, tile(zo, xl), 4, to_r)
        arrived(n, 6, tile(zo, xr), 8)
        send(n, 8, tile(zo, xr) + 4, 4, to_l)

    def complete(n):
        arrived(n, 3, tile(zh, xo), 4)
        arrived(n, 4, tile(zh, xo) + 4, 4)
        arrived(n, 7, tile(zo, xo), 4)
        arrived(n, 8, tile(zo, xo) + 4, 4)

    def work(n):
        complete(n)
        ladder(n)
        exchange(n)

    for n in range(CHUNKS):
        if n:
            masked(n)
        own_z(n)
        own_x(n)
    for peer in y_peers:
        pl.semaphore_signal(met, inc=1, device_id=peer, device_id_type=MESH)

    def grid(shape, axis):
        return lax.broadcasted_iota(jnp.int32, shape, axis)

    i, j = grid((GROUP, GROUP), 0), grid((GROUP, GROUP), 1)
    to_send = lax.rem(i // BLK, P_LOCAL) * (RUN) + (i // PACK) * BLK + lax.rem(i, BLK)
    turn[...] = jnp.where(j == to_send, 1.0, 0.0).astype(BF16)
    i, j = grid((TILE, TILE), 0), grid((TILE, TILE), 1)
    back = jnp.where(i + j == TILE - 1, 1.0, 0.0).astype(BF16)
    loads[CHUNKS + 1].wait()
    total = NZL * PEERS * BLK
    i, j = grid((total, NZL * PEERS), 0), grid((total, NZL * PEERS), 1)
    spread = jnp.where(i // BLK == j, 1.0, 0.0).astype(BF16)
    each = lax.dot_general(
        spread, slot[...].astype(F32).astype(BF16), (((1,), (1,)), ((), ())), preferred_element_type=F32
    )
    i, j = grid((total, BLK), 0), grid((total, BLK), 1)
    column = jnp.sum(jnp.where(lax.rem(i, BLK) == j, each, 0.0), axis=1, keepdims=True)
    slot_wide[...] = jnp.broadcast_to(column, (total, TILE))
    for n in range(CHUNKS):
        for g, group in enumerate(groups(n)):
            part = slot_wide[pl.ds(pl.multiple_of(group * RUN, RUN), RUN), :]
            for half in range(2):
                i, j = grid((RUN, TILE), 0), grid((RUN, TILE), 1)
                offset = (j + half * TILE - (i // BLK) * PACK).astype(F32) - part
                for p in range(P_LOCAL):
                    swap[FIRST[n] + g, p * RUN : (p + 1) * RUN, half * TILE : (half + 1) * TILE] = (
                        jnp.where(offset == float(p * BLK), 1.0, 0.0).astype(BF16)
                    )
    loads[CHUNKS + 2].wait()
    loads[CHUNKS + 3].wait()

    def ladder(n):
        size = len(PLAN[n][1])

        def one(p, carry):
            left = jnp.concatenate([xs[n][rows[p, k]] for k in range(DEG)], axis=1)
            acc = jnp.dot(left, weights[p], preferred_element_type=F32).astype(BF16)
            at = pl.ds(pl.multiple_of(p * RUN, RUN), RUN)
            for g in range(size):
                lad[FIRST[n] + g, at, :] = acc[g * RUN : (g + 1) * RUN]
            return carry

        lax.fori_loop(0, P_LOCAL, one, 0, unroll=8)
        for g in range(FIRST[n], FIRST[n] + size):
            packed = jnp.dot(turn[...], lad[g], preferred_element_type=F32).astype(BF16)
            sent[g * HALF : (g + 1) * HALF] = packed.reshape(HALF, PACK, TILE)

    def exchange(n):
        size, base = len(PLAN[n][1]) * HALF, FIRST[n] * HALF
        place = mine if size == PEERS else lax.rem(mine, HALF)
        own_group = PLAN[n][0] == 0 and 0 in PLAN[n][1]
        for i in range(1 if own_group else 0, size):
            at = lax.rem(place + i, size) if own_group else i
            peer = (first_group(n) * HALF + at, virt)
            remote(sent.at[base + at], got.at[base + place], ms.at[n], mr.at[n], peer).start()
        if own_group:
            got[base + place] = sent[base + place]

    def bytes_of(n):
        size, base = len(PLAN[n][1]) * HALF, FIRST[n] * HALF
        own_group = PLAN[n][0] == 0 and 0 in PLAN[n][1]
        part = pl.ds(base, size - 1 if own_group else size)
        return remote(sent.at[part], got.at[part], ms.at[n], mr.at[n], to_z)

    def combine(n):
        bytes_of(n).wait_recv()
        for g, group in enumerate(groups(n)):
            g += FIRST[n]
            block = got[g * HALF : (g + 1) * HALF].reshape(GROUP, TILE)
            mirrored = jnp.dot(swap[g], block, preferred_element_type=F32).astype(BF16)
            mirrored = jnp.dot(mirrored, back, preferred_element_type=F32)
            both = (lad[g].astype(F32) + mirrored).astype(BF16)
            start = pl.multiple_of(group * RUN, RUN)
            for p in range(P_LOCAL):
                out[pl.ds(start, RUN), p * TILE : (p + 1) * TILE] = both[p * RUN : (p + 1) * RUN]

    pl.semaphore_wait(met, len(y_peers))
    for step in range(CHUNKS + 4):
        if step < CHUNKS:
            pass_own(step)
        if 0 <= step - 1 < CHUNKS:
            cross(step - 1)
        if 0 <= step - 2 < CHUNKS:
            forward(step - 2)
        if 0 <= step - 3 < CHUNKS:
            work(step - 3)
    for copy in pending:
        copy.wait_send()
    for n in range(CHUNKS):
        combine(n)
    for n in range(CHUNKS):
        bytes_of(n).wait_send()


def on_device(amplitudes, amp_mask, integrals, int_rows, mirror_slot):
    hbm = pl.BlockSpec(memory_space=pl.ANY)
    total = NZL * PEERS * BLK
    return pl.pallas_call(
        kernel,
        out_shape=pltpu.VMEM((total, P_LOCAL * TILE), BF16),
        in_specs=[hbm] * 5,
        out_specs=pl.BlockSpec(memory_space=pltpu.VMEM),
        scratch_shapes=[pltpu.VMEM((NX * NZH * Q_LOCAL, RUN * len(c[1]), TILE), BF16) for c in PLAN]
        + [pltpu.VMEM((RUN * len(c[1]), Q_LOCAL * TILE), BF16) for c in PLAN]
        + [
            pltpu.VMEM((GROUPS, GROUP, TILE), BF16),
            pltpu.VMEM((GROUPS * HALF, PACK, TILE), BF16),
            pltpu.VMEM((GROUPS * HALF, PACK, TILE), BF16),
            pltpu.VMEM((Q_LOCAL, total), jnp.int32),
            pltpu.VMEM((P_LOCAL, DEG * TILE, TILE), BF16),
            pltpu.SMEM((P_LOCAL, DEG), jnp.int32),
            pltpu.VMEM((BLK, NZL * PEERS), jnp.int32),
            pltpu.VMEM((GROUP, GROUP), BF16),
            pltpu.VMEM((GROUPS, GROUP, GROUP), BF16),
            pltpu.VMEM((total, TILE), F32),
            pltpu.VMEM((total, Q_LOCAL), F32),
            pltpu.SemaphoreType.DMA((CHUNKS + 4,)),
            pltpu.SemaphoreType.DMA((CHUNKS, 9)),
            pltpu.SemaphoreType.DMA((CHUNKS, 9)),
            pltpu.SemaphoreType.DMA((CHUNKS,)),
            pltpu.SemaphoreType.DMA((CHUNKS,)),
            pltpu.SemaphoreType.REGULAR,
        ],
        compiler_params=pltpu.CompilerParams(
            collective_id=0, has_side_effects=True, vmem_limit_bytes=40 << 20
        ),
        name="ladder",
    )(
        *(
            pltpu.with_memory_space_constraint(a, pltpu.HBM)
            for a in (
                amplitudes,
                amp_mask.T,
                integrals.reshape(P_LOCAL, DEG * TILE, TILE),
                int_rows,
                mirror_slot.T,
            )
        )
    )


def solution(mesh):
    placed = (
        P("pair", "virt"),
        P("pair", "virt"),
        P("virt", None, None, None),
        P("virt", None),
        P("pair", None),
    )
    return jax.shard_map(
        on_device, mesh=mesh, in_specs=placed, out_specs=P("pair", "virt"), check_vma=False
    )
```

time: 65.4 us -> 59.6 us (0.911)
  Pallas kernels: 64.4 us -> 58.1 us
    pallas_call x1, Pallas kernels: 64.4 us -> 58.1 us  [on_device(): pl.pallas_call(kernel, out_shape=pltpu.VMEM((total, P_LOCAL * TILE), BF16...]
where the time goes in v3:
time: 59.6 us; the launch traced here: 58.9 us
  Pallas kernels  58.1 us (97%)
  local copies, waits for them, and re-layouts  0.8 us (1%)
    pallas_call x1, Pallas kernels, on_device(): pl.pallas_call(kernel, out_shape=pltpu.VMEM((total, P_LOCAL * TILE), BF16...  58.1 us

profile of v3, /device:TPU:1, one launch (start us, length us, event | category | flops | bytes accessed | tf_op | source)
XLA Modules:
  0.0 58.9 jit_solution(4838659087876800789)
XLA Ops:
  0.0 58.1 %ladder.1 = bf16[256,1024]{1,0:T(8,128)(2,1)S(1)} custom-call(bf16[256,1024]{1,0:T(8,128)(2,1)} %amp_hbm.1, s32[8,256]{1,0:T(8,128)} %bitcast.4, bf16[8,1536,128]{2,1,0:T(8,128)(2,1)} %bitcast.3, s32[8,12]{1,0:T(8,128)} %rows_hbm.1, s32[4,64]{1,0:T(4,128)} %bitcast.5), custom_call_target="tpu_custom_call" | custom-call | tf_op jit(solution)/shard_map/ladder/pallas_call | solution.py:257
  58.1 0.8 %copy.7 = bf16[256,1024]{1,0:T(8,128)(2,1)} copy(bf16[256,1024]{1,0:T(8,128)(2,1)S(1)} %ladder.1) | data formatting | bytes 1048576

commit v4 on v3

--- a/solution.py
+++ b/solution.py
@@ -18,7 +18,7 @@
 GROUP = RUN * P_LOCAL
 PACK = P_LOCAL * BLK
 GROUPS = NZL * PEERS // HALF
-PLAN = ((3, (0, 1)), (2, (0, 1)), (1, (0, 1)), (0, (1,)), (0, (0,)))
+PLAN = ((2, (0, 1)), (3, (0, 1)), (1, (0, 1)), (0, (1,)), (0, (0,)))
 CHUNKS = len(PLAN)
 FIRST = [sum(len(c[1]) for c in PLAN[:n]) for n in range(CHUNKS)]
 
@@ -152,7 +152,8 @@
     for n in range(CHUNKS):
         if n:
             masked(n)
-        own_z(n)
+        if n == 0:
+            own_z(n)
         own_x(n)
     for peer in y_peers:
         pl.semaphore_signal(met, inc=1, device_id=peer, device_id_type=MESH)
@@ -236,6 +237,8 @@
     pl.semaphore_wait(met, len(y_peers))
     for step in range(CHUNKS + 4):
         if step < CHUNKS:
+            if step + 1 < CHUNKS:
+                own_z(step + 1)
             pass_own(step)
         if 0 <= step - 1 < CHUNKS:
             cross(step - 1)

time: 59.6 us -> 58.7 us (0.985)
  no operation moved by 1% of the time
where the time goes in v4:
time: 58.7 us; the launch traced here: 58.6 us
  Pallas kernels  57.8 us (98%)
  local copies, waits for them, and re-layouts  0.8 us (1%)
    pallas_call x1, Pallas kernels, on_device(): pl.pallas_call(kernel, out_shape=pltpu.VMEM((total, P_LOCAL * TILE), BF16...  57.8 us

profile of v4, /device:TPU:1, one launch (start us, length us, event | category | flops | bytes accessed | tf_op | source)
XLA Modules:
  0.0 58.6 jit_solution(795641582515793454)
XLA Ops:
  0.0 57.8 %ladder.1 = bf16[256,1024]{1,0:T(8,128)(2,1)S(1)} custom-call(bf16[256,1024]{1,0:T(8,128)(2,1)} %amp_hbm.1, s32[8,256]{1,0:T(8,128)} %bitcast.4, bf16[8,1536,128]{2,1,0:T(8,128)(2,1)} %bitcast.3, s32[8,12]{1,0:T(8,128)} %rows_hbm.1, s32[4,64]{1,0:T(4,128)} %bitcast.5), custom_call_target="tpu_custom_call" | custom-call | tf_op jit(solution)/shard_map/ladder/pallas_call | solution.py:260
  57.8 0.8 %copy.7 = bf16[256,1024]{1,0:T(8,128)(2,1)} copy(bf16[256,1024]{1,0:T(8,128)(2,1)S(1)} %ladder.1) | data formatting | bytes 1048576

commit v5 on v4

--- a/solution.py
+++ b/solution.py
@@ -69,18 +69,20 @@
         for i in range(1, NZL * NC)
     ]
     first = [to_r, to_l, to_z] + z_peers + y_peers
-    for peer in first:
-        pl.semaphore_signal(barrier, inc=1, device_id=peer, device_id_type=MESH)
-
     loads = [pltpu.make_async_copy(mask_hbm, mask, load_sem.at[0])]
     for n in range(CHUNKS):
         loads.append(pltpu.make_async_copy(amp_hbm.at[rows_of(n)], amps[n], load_sem.at[1 + n]))
     loads.append(pltpu.make_async_copy(slot_hbm, slot, load_sem.at[CHUNKS + 1]))
     loads.append(pltpu.make_async_copy(rows_hbm, rows, load_sem.at[CHUNKS + 2]))
     loads.append(pltpu.make_async_copy(int_hbm, weights, load_sem.at[CHUNKS + 3]))
-    for load in loads:
+
+    for load in loads[:3]:
         load.start()
-
+    for peer in first:
+        pl.semaphore_signal(barrier, inc=1, device_id=peer, device_id_type=MESH)
+
+    for load in loads[3:]:
+        load.start()
     pending = []
 
     def gather(n, i, first_tile, tiles):

time: 58.7 us -> 58.7 us (level)
  no operation moved by 1% of the time
where the time goes in v5:
time: 58.7 us; the launch traced here: 58.5 us
  Pallas kernels  57.7 us (98%)
  local copies, waits for them, and re-layouts  0.8 us (1%)
    pallas_call x1, Pallas kernels, on_device(): pl.pallas_call(kernel, out_shape=pltpu.VMEM((total, P_LOCAL * TILE), BF16...  57.7 us

profile of v5, /device:TPU:1, one launch (start us, length us, event | category | flops | bytes accessed | tf_op | source)
XLA Modules:
  0.0 58.5 jit_solution(18103704865513490502)
XLA Ops:
  0.0 57.7 %ladder.1 = bf16[256,1024]{1,0:T(8,128)(2,1)S(1)} custom-call(bf16[256,1024]{1,0:T(8,128)(2,1)} %amp_hbm.1, s32[8,256]{1,0:T(8,128)} %bitcast.4, bf16[8,1536,128]{2,1,0:T(8,128)(2,1)} %bitcast.3, s32[8,12]{1,0:T(8,128)} %rows_hbm.1, s32[4,64]{1,0:T(4,128)} %bitcast.5), custom_call_target="tpu_custom_call" | custom-call | tf_op jit(solution)/shard_map/ladder/pallas_call | solution.py:262
  57.7 0.8 %copy.7 = bf16[256,1024]{1,0:T(8,128)(2,1)} copy(bf16[256,1024]{1,0:T(8,128)(2,1)S(1)} %ladder.1) | data formatting | bytes 1048576
